TPU v7x, 256 devices: a whole 4x4x8 slice. The times are simulated.
256 devices in a mesh: ctx: 32 (over z_hi, y, core), mp: 8 (over x, z_lo).
Axes of the slice: x: 4, y: 4, z: 8 (z_hi: 4, z_lo: 2; z = z_hi * 2 + z_lo), core: 2. Of those that a mesh axis runs over, the one named last changes fastest.
Arguments:
- query_rows: bfloat16 [5120, 5120], P('ctx', 'mp'), may hold values from -42 to 42
- key_rows: bfloat16 [5120, 1024], P('ctx', 'mp'), may hold values from -42 to 42
- value_matrix: bfloat16 [5120, 1024], P('ctx', 'mp'), may hold values from -6 to 6
- cotangent: bfloat16 [5120, 5120], P('ctx', 'mp'), may hold values from -6 to 6
- frozen_out: bfloat16 [5120, 5120], P('mp'), may hold values from -0.078125 to 0.078125
- adapter_down: bfloat16 [5120, 64], P('mp'), may hold values from -0.078125 to 0.078125
- adapter_up: bfloat16 [64, 5120], replicated, may hold values from -0.0390625 to 0.0390625
- doc_lengths: int32 [4], replicated, may hold values from 1 to 2560, 5120 in all
Outputs:
- query_grads: bfloat16 [5120, 5120], P('ctx', 'mp')
- key_gradient: bfloat16 [5120, 1024], P('ctx', 'mp')
- value_gradient: bfloat16 [5120, 1024], P('ctx', 'mp')
- down_grad: float32 [5120, 64], P('mp')
- up_grad: float32 [64, 5120], P(None, 'mp')
Inputs may be any that keep to these rules, and one draw needn't show every extreme that they name: `doc_lengths`: the 4 documents fill the window in order, their lengths sum to 5120, and the longest is exactly half of 5120 long.
All inputs are finite; a program needn't handle non-finite values.
Results may differ from a plain program's by a relative error of at most 0.04.
Values may be sent and summed in bfloat16 or wider, within the bound.
A program may use at most 64 MiB of HBM per device.

v0:
```python
import functools
import math

import jax
import jax.numpy as jnp
from jax import lax
from jax.experimental import pallas as pl
from jax.experimental.pallas import tpu as pltpu
from jax.sharding import PartitionSpec as P

HEAD_SIZE = 128
T = 160
GROUP = 5
N = 896
FEATURES = 640
RANK = 64
SLOTS = 17
SCALE = HEAD_SIZE**-0.5
EXP_SCALE = SCALE * math.log2(math.e)
GAIN = 2.0
MASKED = -1e30
MESH = pl.DeviceIdType.MESH
F32 = jnp.float32
BF16 = jnp.bfloat16
PIECE = 2 * RANK // 8

KV = 0
COT = 16
SIB = 30
COL = 46
DEEP = 58
RK = 62
DU = 69
DU_Z = 76
DU_BACK = 79
MESSAGES = 86


def dot(left, right, left_dim, right_dim):
    return lax.dot_general(
        left, right, (((left_dim,), (right_dim,)), ((), ())), preferred_element_type=F32
    )


def kernel(
    lengths, q_hbm, k_hbm, v_hbm, cot_hbm, w_hbm, up_hbm, down_hbm,
    dq_out, dk_out, dv_out, down_out, up_out,
    kv, cots, w, down, qs, scores, probs, dos, doc, acc, parts, sib, col, deep, own,
    rank_in, du, du_in, du_z, du_sum, dq_v, dkv_v, du_v, send_sem, recv_sem, load_sem,
):
    i = lax.axis_index("ctx")
    mp = lax.axis_index("mp")
    h, y, c = i // 8, (i // 2) % 4, i % 2
    x, zl = mp // 2, mp % 2
    other = 1 - c

    def at(dh=0, dy=0, core=None):
        return (
            ((h + dh + 4) % 4) * 8 + ((y + dy + 4) % 4) * 2 + (c if core is None else core),
            mp,
        )

    def along(dx=0, z=None):
        return (i, ((x + dx + 4) % 4) * 2 + (zl if z is None else z))

    def slot(kind, yy, cc):
        return kind * 8 + cc * 4 + yy

    sent = []

    def message_to(src, dst, message, device):
        copy = pltpu.make_async_remote_copy(
            src_ref=src, dst_ref=dst, send_sem=send_sem.at[len(sent)], recv_sem=recv_sem.at[message],
            device_id=device, device_id_type=MESH,
        )
        sent.append(copy)
        return copy

    def send(src, dst, message, device):
        message_to(src, dst, message, device).start()

    def arrived(dst, message):
        pltpu.make_async_remote_copy(
            src_ref=dst, dst_ref=dst, send_sem=send_sem.at[0], recv_sem=recv_sem.at[message],
            device_id=at(core=other), device_id_type=MESH,
        ).wait_recv()

    for kind in (0, 1):
        kv[slot(kind, y, c)] = jnp.zeros((T, 2 * HEAD_SIZE), BF16)
    barrier = pltpu.get_barrier_semaphore()
    plane = [(d, cc) for d in (0, 1, 2, 3) for cc in (0, 1) if (d, cc) != (0, 0)]
    ranks = [along(dx=d) for d in (1, 2, 3)] + [along(dx=d, z=1 - zl) for d in (0, 1, 2, 3)]
    partners = [at(dh=d) for d in (2, 1, 3)] + ranks + [at(dy=d, core=(c + cc) % 2) for d, cc in plane]
    for partner in partners:
        pl.semaphore_signal(barrier, inc=1, device_id=partner, device_id_type=MESH)

    loads = []

    def load(src, dst):
        loads.append(pltpu.make_async_copy(src, dst, load_sem.at[len(loads)]))
        loads[-1].start()

    load(k_hbm, kv.at[16, :, pl.ds(0, HEAD_SIZE)])
    load(v_hbm, kv.at[16, :, pl.ds(HEAD_SIZE, HEAD_SIZE)])
    load(cot_hbm, cots.at[mp])
    qs[T * GROUP : N, :] = jnp.zeros((N - T * GROUP, HEAD_SIZE), BF16)
    for copy in loads[0:3]:
        copy.wait()
    pl.semaphore_wait(barrier, len(partners))

    g1, mix = slot(0, y, c), slot(1, y, c)
    near = x * 2 + 1 - zl
    left, right, far = ((x + 3) % 4) * 2, ((x + 1) % 4) * 2, ((x + 2) % 4) * 2
    half0, half1 = pl.ds(0, T // 2), pl.ds(T // 2, T // 2)
    halves = (half0, half1)

    def half(block, n):
        return cots.at[block, halves[n]]

    limited = []

    def send_if(condition, src, dst, message, device):
        copy = message_to(src, dst, message, device)
        limited.append((condition, sent.pop()))
        sent.append(None)
        pl.when(condition)(copy.start)

    send_if(h < 3, kv.at[16], kv.at[g1], KV + g1, at(dh=1))
    send_if(h < 2, kv.at[16], kv.at[mix], KV + mix, at(dh=2))
    for n in (0, 1):
        send(half(mp, n), half(mp, n), COT + 2 + n, along(dx=1))
        send(half(mp, 1 - n), half(mp, 1 - n), COT + 5 - n, along(dx=-1))
    send(half(mp, 0), half(mp, 0), COT + 0, along(z=1 - zl))
    send(half(mp, 1), half(mp, 1), COT + 1, along(z=1 - zl))
    early, late = [], []
    for d in (1, 2, 3):
        copy = message_to(kv.at[16], kv.at[mix], KV + mix, at(dy=d))
        early.append((y + d < 4, copy))
        late.append((y + d >= 4, pltpu.make_async_remote_copy(
            src_ref=kv.at[mix], dst_ref=kv.at[mix], send_sem=send_sem.at[len(sent) - 1],
            recv_sem=recv_sem.at[KV + mix], device_id=at(dy=d), device_id_type=MESH)))
    copy = message_to(kv.at[16], kv.at[mix], KV + mix, at(core=other))
    early.append((c == 0, copy))
    late.append((c == 1, pltpu.make_async_remote_copy(
        src_ref=kv.at[mix], dst_ref=kv.at[mix], send_sem=send_sem.at[len(sent) - 1],
        recv_sem=recv_sem.at[KV + mix], device_id=at(core=other), device_id_type=MESH)))
    for condition, copy in early:
        pl.when(condition)(copy.start)

    for g in range(GROUP):
        load(q_hbm.at[:, pl.ds(HEAD_SIZE * g, HEAD_SIZE)], qs.at[pl.ds(T * g, T)])
    load(down_hbm, down)
    for b in range(8):
        load(w_hbm.at[:, pl.ds(FEATURES * b, FEATURES)], w.at[b, pl.ds(0, FEATURES)])
        load(up_hbm.at[:, pl.ds(FEATURES * b, FEATURES)], w.at[b, pl.ds(FEATURES, RANK)])

    token = lax.broadcasted_iota(jnp.int32, (1, N), 1)
    for g in range(GROUP):
        token = token - jnp.where(token >= T, T, 0)
    position = token + i * T
    end0 = lengths[0]
    end1 = end0 + lengths[1]
    end2 = end1 + lengths[2]
    start = jnp.where(
        position >= end2, end2, jnp.where(position >= end1, end1, jnp.where(position >= end0, end0, 0))
    )
    row = lax.broadcasted_iota(jnp.int32, (T, N), 0)

    def forward(first, count, bases, state, causal=False):
        keys = kv[pl.ds(first, count), :, 0:HEAD_SIZE].reshape(count * T, HEAD_SIZE)
        values = kv[pl.ds(first, count), :, HEAD_SIZE:].reshape(count * T, HEAD_SIZE)
        raw = dot(keys, qs[...], 1, 1).reshape(count, T, N)
        top = jnp.full((8, N), MASKED, F32)
        for s in range(count):
            allowed = row >= start - bases[s]
            if causal:
                allowed = allowed & (row <= token)
            block = jnp.where(allowed, raw[s], MASKED)
            scores[s] = block
            top = jnp.maximum(top, jnp.max(block.reshape(T // 8, 8, N), axis=0))
        peak = jnp.max(top, axis=0, keepdims=True) * EXP_SCALE
        if state is not None:
            peak = jnp.maximum(peak, state[0])
        weights = jnp.exp2(scores[0:count].reshape(count * T, N) * EXP_SCALE - peak)
        total = jnp.sum(weights.reshape(count * T // 8, 8, N), axis=0)
        low = weights.astype(BF16)
        probs[pl.ds(first, count)] = low.reshape(count, T, N)
        out_t = dot(values, low, 0, 0)
        if state is not None:
            decay = jnp.exp2(state[0] - peak)
            total = total + state[1] * decay
            out_t = out_t + state[2] * decay
        return peak, total, out_t

    def bases_of(kind, cc):
        out = []
        for yy in range(4):
            j = 2 * yy + cc
            if kind == 0:
                group = h - 1
            else:
                group = jnp.where(j < 2 * y + c, h, h - 2)
            out.append((8 * group + j) * T)
        return out

    def project(block):
        acc[...] += dot(cots[block], w[block], 1, 1)

    for copy in loads[3:8]:
        copy.wait()
    peaks = {}
    state = forward(16, 1, [i * T], None, causal=True)
    peaks["own"] = state[0]

    arrived(half(left + zl, 0), COT + 2)
    send(half(left + zl, 0), half(left + zl, 0), COT + 6, along(dx=1))
    arrived(half(right + zl, 1), COT + 5)
    send(half(right + zl, 1), half(right + zl, 1), COT + 7, along(dx=-1))
    pl.when(h >= 1)(lambda: arrived(kv.at[g1], KV + g1))
    for d in (1, 2, 3):
        send(kv.at[g1], kv.at[g1], KV + g1, at(dy=d))
    send(kv.at[g1], kv.at[g1], KV + g1, at(core=other))
    pl.when(h >= 2)(lambda: arrived(kv.at[mix], KV + mix))
    for condition, copy in late:
        pl.when(condition)(copy.start)
    arrived(half(near, 0), COT + 0)
    send(half(near, 0), half(near, 0), COT + 8, along(dx=1))
    arrived(half(near, 1), COT + 1)
    send(half(near, 1), half(near, 1), COT + 11, along(dx=-1))
    send(half(near, 1), half(near, 1), COT + 9, along(dx=1))
    send(half(near, 0), half(near, 0), COT + 10, along(dx=-1))
    for copy in loads[8:]:
        copy.wait()
    acc[...] = dot(cots[mp], w[mp], 1, 1)
    project(near)

    for kind in (0, 1):
        for d in (1, 2, 3):
            s = slot(kind, (y + d) % 4, c)
            arrived(kv.at[s], KV + s)
            send(kv.at[s], kv.at[s], KV + s, at(core=other))
        state = forward(slot(kind, 0, c), 4, bases_of(kind, c), state)
        peaks[kind, 0] = state[0]
        if kind == 0:
            arrived(half(left + 1 - zl, 0), COT + 8)
            send(half(left + 1 - zl, 0), half(left + 1 - zl, 0), COT + 12, along(dx=1))
            arrived(half(right + 1 - zl, 1), COT + 11)
            send(half(right + 1 - zl, 1), half(right + 1 - zl, 1), COT + 13, along(dx=-1))

    arrived(half(left + zl, 1), COT + 3)
    arrived(half(right + zl, 0), COT + 4)
    for block in (left + zl, right + zl):
        project(block)
    for kind in (0, 1):
        for yy in range(4):
            s = slot(kind, yy, other)
            arrived(kv.at[s], KV + s)
        state = forward(slot(kind, 0, other), 4, bases_of(kind, other), state)
        peaks[kind, 1] = state[0]

    peak, total, out_t = state
    inverse = 1.0 / jnp.sum(total, axis=0, keepdims=True)
    out_t = (out_t * inverse).astype(BF16).astype(F32)
    out = out_t.T.astype(BF16)

    rank_part = jnp.zeros((T, RANK), F32)
    for g in range(GROUP):
        rank_part = rank_part + dot(
            out[T * g : T * (g + 1)], down[:, HEAD_SIZE * g : HEAD_SIZE * (g + 1)], 1, 1
        )
    rank_in[0] = jnp.concatenate([rank_part[: T // 2], rank_part[T // 2 :]], axis=1).astype(BF16)
    for n, device in enumerate(ranks):
        send(rank_in.at[0], rank_in.at[1 + n], RK + n, device)

    arrived(half(left + 1 - zl, 1), COT + 9)
    project(left + 1 - zl)
    arrived(half(right + 1 - zl, 0), COT + 10)
    project(right + 1 - zl)
    arrived(half(far + zl, 0), COT + 6)
    arrived(half(far + zl, 1), COT + 7)
    project(far + zl)
    arrived(half(far + 1 - zl, 0), COT + 12)
    arrived(half(far + 1 - zl, 1), COT + 13)
    project(far + 1 - zl)
    rank_grad = acc[:, FEATURES:].astype(BF16)
    out_grad = (acc[:, 0:FEATURES] + GAIN * dot(rank_grad, down[...], 1, 0)).astype(BF16).astype(F32)
    for g in range(GROUP):
        dos[T * g : T * (g + 1), :] = out_grad[:, HEAD_SIZE * g : HEAD_SIZE * (g + 1)]
    dos[T * GROUP : N, :] = jnp.zeros((N - T * GROUP, HEAD_SIZE), F32)
    do_t = dos[...].T * inverse
    delta = jnp.sum(do_t * out_t, axis=0, keepdims=True)

    chunks = [("own", 16, 1)]
    chunks += [((kind, k), slot(kind, 0, c if k == 0 else other), 4) for k in (1, 0) for kind in (1, 0)]
    deltas, place = {}, {}
    for n, (key, first, count) in enumerate(chunks):
        factor = jnp.exp2(peaks[key] - peak)
        doc[n] = (do_t * factor).astype(BF16)
        deltas[key] = delta * factor
        place[key] = n

    def value_part(key, first, count):
        low = probs[pl.ds(first, count)].reshape(count * T, N)
        dv = dot(low, doc[place[key]], 1, 1)
        if count == 1:
            own[1] = dv
        else:
            parts[1, pl.ds(first, count)] = dv.astype(BF16).reshape(count, T, HEAD_SIZE)

    def key_part(key, first, count, dq_t):
        keys = kv[pl.ds(first, count), :, 0:HEAD_SIZE].reshape(count * T, HEAD_SIZE)
        values = kv[pl.ds(first, count), :, HEAD_SIZE:].reshape(count * T, HEAD_SIZE)
        low = probs[pl.ds(first, count)].reshape(count * T, N)
        dprob = dot(values, doc[place[key]], 1, 0)
        dscore = (low.astype(F32) * (dprob - deltas[key])).astype(BF16)
        dk = dot(dscore, qs[...], 1, 0) * SCALE
        if count == 1:
            own[0] = dk
        else:
            parts[0, pl.ds(first, count)] = dk.astype(BF16).reshape(count, T, HEAD_SIZE)
        return dq_t + dot(keys, dscore, 0, 0)

    def to_other_core(kv_of, kind):
        for yy in range(4):
            n = 4 * kind + yy
            send(parts.at[kv_of, slot(kind, yy, other)], sib.at[kv_of, n], SIB + 8 * kv_of + n, at(core=other))

    def along_y(kv_of, kind):
        for yy in range(4):
            n = 4 * kind + yy
            arrived(sib.at[kv_of, n], SIB + 8 * kv_of + n)
        for d in (1, 2, 3):
            yy = (y + d) % 4
            s = slot(kind, yy, c)
            parts[kv_of, s] = (parts[kv_of, s].astype(F32) + sib[kv_of, 4 * kind + yy].astype(F32)).astype(BF16)
            n = 6 * kv_of + 3 * kind + d - 1
            send(parts.at[kv_of, s], col.at[n], COL + n, at(dy=d))
        term = sib[kv_of, 4 * kind + y].astype(F32)
        if kind == 0:
            parts[kv_of, g1] = (parts[kv_of, g1].astype(F32) + term).astype(BF16)
        else:
            own[kv_of] += term * (1 - c).astype(F32)
            parts[kv_of, mix] = (parts[kv_of, mix].astype(F32) + term * c.astype(F32)).astype(BF16)

    def along_z(kv_of, kind):
        s = mix if kind == 1 else g1
        total = parts[kv_of, s].astype(F32)
        for d in (1, 2, 3):
            n = 6 * kv_of + 3 * kind + d - 1
            arrived(col.at[n], COL + n)
            term = col[n].astype(F32)
            if kind == 1:
                later = jnp.where(y - d < 0, 1.0, 0.0)
                own[kv_of] += term * later
                term = term * (1.0 - later)
            total = total + term
        parts[kv_of, s] = total.astype(BF16)
        n = 2 * kv_of + kind
        send_if(h >= 1 + kind, parts.at[kv_of, s], deep.at[n], DEEP + n, at(dh=-1 - kind))

    by_key = {key: (key, first, count) for key, first, count in chunks}
    for kind in (1, 0):
        value_part(*by_key[kind, 1])
        to_other_core(1, kind)
    value_part(*by_key["own"])
    for kind in (1, 0):
        value_part(*by_key[kind, 0])

    for n in range(7):
        arrived(rank_in.at[1 + n], RK + n)
    rank_sum = rank_in[0].astype(F32)
    for n in range(7):
        rank_sum = rank_sum + rank_in[1 + n].astype(F32)
    rank_acts = jnp.concatenate([rank_sum[:, :RANK], rank_sum[:, RANK:]], axis=0).astype(BF16)
    for g in range(GROUP):
        du[0:RANK, HEAD_SIZE * g : HEAD_SIZE * (g + 1)] = (
            GAIN * dot(rank_grad, out[T * g : T * (g + 1)], 0, 0)
        ).astype(BF16)
    du[RANK:, :] = (GAIN * dot(rank_acts, cots[mp], 0, 0)).astype(BF16)

    def piece(yy, cc):
        return pl.ds((yy * 2 + cc) * PIECE, PIECE)

    for n, (d, cc) in enumerate(plane):
        yy, core = (y + d) % 4, (c + cc) % 2
        send(du.at[piece(yy, core)], du_in.at[n], DU + n, at(dy=d, core=core))

    for kind in (1, 0):
        along_y(1, kind)
    dq_t = key_part(*by_key["own"], jnp.zeros((HEAD_SIZE, N), F32))
    for kind in (1, 0):
        dq_t = key_part(*by_key[kind, 1], dq_t)
        to_other_core(0, kind)

    total_du = du[piece(y, c)].astype(F32)
    for n in range(7):
        arrived(du_in.at[n], DU + n)
        total_du = total_du + du_in[n].astype(F32)
    du_z[3] = total_du.astype(BF16)
    for d in (1, 2, 3):
        send(du_z.at[3], du_z.at[d - 1], DU_Z + d - 1, at(dh=d))

    for kind in (1, 0):
        along_z(1, kind)
    for kind in (1, 0):
        dq_t = key_part(*by_key[kind, 0], dq_t)
        along_y(0, kind)

    for d in (1, 2, 3):
        arrived(du_z.at[d - 1], DU_Z + d - 1)
        total_du = total_du + du_z[d - 1].astype(F32)
    du_sum[piece(y, c)] = total_du.astype(BF16)
    for n, (d, cc) in enumerate(plane):
        send(du_sum.at[piece(y, c)], du_sum.at[piece(y, c)], DU_BACK + n, at(dy=d, core=(c + cc) % 2))

    results = []

    def store(src, dst):
        results.append(pltpu.make_async_copy(src, dst, load_sem.at[len(loads) + len(results)]))
        results[-1].start()

    for kind in (1, 0):
        along_z(0, kind)

    dq = (dq_t * SCALE).T.astype(BF16)
    for g in range(GROUP):
        dq_v[:, HEAD_SIZE * g : HEAD_SIZE * (g + 1)] = dq[T * g : T * (g + 1), :]
    store(dq_v, dq_out)

    for n, (d, cc) in enumerate(plane):
        arrived(du_sum.at[piece((y - d + 4) % 4, (c + cc) % 2)], DU_BACK + n)
    du_v[...] = du_sum[...].astype(F32)
    store(du_v.at[pl.ds(0, RANK)], down_out)
    store(du_v.at[pl.ds(RANK, RANK)], up_out)

    def add_deep(kv_of, kind):
        n = 2 * kv_of + kind
        arrived(deep.at[n], DEEP + n)
        own[kv_of] += deep[n].astype(F32)

    for kv_of, result in ((1, dv_out), (0, dk_out)):
        for kind in (1, 0):
            pl.when(h < 3 - kind)(functools.partial(add_deep, kv_of, kind))
        dkv_v[kv_of] = own[kv_of].astype(BF16)
        store(dkv_v.at[kv_of], result)
    for copy in sent:
        if copy is not None:
            copy.wait_send()
    for condition, copy in limited:
        pl.when(condition)(copy.wait_send)
    for copy in results:
        copy.wait()


def hand_on(*refs):
    sources, results, held, sems = refs[0:5], refs[5:10], refs[10:15], refs[15]
    copies = [pltpu.make_async_copy(sources[n], held[n], sems.at[n]) for n in range(5)]
    for copy in copies:
        copy.start()
    outs = [pltpu.make_async_copy(held[n], results[n], sems.at[5 + n]) for n in range(5)]
    for n in (1, 2, 0, 3, 4):
        copies[n].wait()
        outs[n].start()
    for copy in outs:
        copy.wait()


def body(query_rows, key_rows, value_matrix, cotangent, frozen_out, adapter_down, adapter_up, doc_lengths):
    hbm = pl.BlockSpec(memory_space=pl.ANY)
    shapes = (
        jax.ShapeDtypeStruct((T, FEATURES), BF16),
        jax.ShapeDtypeStruct((T, HEAD_SIZE), BF16),
        jax.ShapeDtypeStruct((T, HEAD_SIZE), BF16),
        jax.ShapeDtypeStruct((RANK, FEATURES), F32),
        jax.ShapeDtypeStruct((RANK, FEATURES), F32),
    )
    outs = pl.pallas_call(
        kernel,
        out_shape=shapes,
        in_specs=[pl.BlockSpec(memory_space=pltpu.SMEM)] + [hbm] * 7,
        out_specs=(hbm,) * 5,
        scratch_shapes=[
            pltpu.VMEM((SLOTS, T, 2 * HEAD_SIZE), BF16),
            pltpu.VMEM((8, T, FEATURES), BF16),
            pltpu.VMEM((8, FEATURES + RANK, FEATURES), BF16),
            pltpu.VMEM((RANK, FEATURES), BF16),
            pltpu.VMEM((N, HEAD_SIZE), BF16),
            pltpu.VMEM((4, T, N), F32),
            pltpu.VMEM((SLOTS, T, N), BF16),
            pltpu.VMEM((N, HEAD_SIZE), F32),
            pltpu.VMEM((5, HEAD_SIZE, N), BF16),
            pltpu.VMEM((T, FEATURES + RANK), F32),
            pltpu.VMEM((2, 16, T, HEAD_SIZE), BF16),
            pltpu.VMEM((2, 8, T, HEAD_SIZE), BF16),
            pltpu.VMEM((12, T, HEAD_SIZE), BF16),
            pltpu.VMEM((4, T, HEAD_SIZE), BF16),
            pltpu.VMEM((2, T, HEAD_SIZE), F32),
            pltpu.VMEM((8, T // 2, 2 * RANK), BF16),
            pltpu.VMEM((2 * RANK, FEATURES), BF16),
            pltpu.VMEM((7, PIECE, FEATURES), BF16),
            pltpu.VMEM((4, PIECE, FEATURES), BF16),
            pltpu.VMEM((2 * RANK, FEATURES), BF16),
            pltpu.VMEM((T, FEATURES), BF16),
            pltpu.VMEM((2, T, HEAD_SIZE), BF16),
            pltpu.VMEM((2 * RANK, FEATURES), F32),
            pltpu.SemaphoreType.DMA((MESSAGES,)),
            pltpu.SemaphoreType.DMA((MESSAGES,)),
            pltpu.SemaphoreType.DMA((32,)),
        ],
        compiler_params=pltpu.CompilerParams(
            collective_id=0, has_side_effects=True, vmem_limit_bytes=60 * 2**20
        ),
    )(
        doc_lengths, query_rows, key_rows, value_matrix, cotangent,
        frozen_out, adapter_up, adapter_down.T,
    )
    dq, dk, dv, down_t, up = pl.pallas_call(
        hand_on,
        out_shape=shapes,
        in_specs=[hbm] * 5,
        out_specs=(hbm,) * 5,
        scratch_shapes=[pltpu.VMEM(shape.shape, shape.dtype) for shape in shapes]
        + [pltpu.SemaphoreType.DMA((10,))],
    )(*outs)
    return dq, dk, dv, down_t.T, up


def solution(mesh):
    return jax.shard_map(
        body,
        mesh=mesh,
        in_specs=(
            P("ctx", "mp"), P("ctx", "mp"), P("ctx", "mp"), P("ctx", "mp"), P("mp", None), P("mp", None), P(), P(),
        ),
        out_specs=(P("ctx", "mp"), P("ctx", "mp"), P("ctx", "mp"), P("mp", None), P(None, "mp")),
        check_vma=False,
    )
```

profile of v0, /device:TPU:1, one launch (start us, length us, event | category | flops | bytes accessed | tf_op | source)
XLA Modules:
  0.0 57.5 jit_solution(2789008490988893346)
XLA Ops:
  0.6 55.0 %shard_map.119 = (bf16[160,640]{1,0:T(8,128)(2,1)}, bf16[160,128]{1,0:T(8,128)(2,1)}, bf16[160,128]{1,0:T(8,128)(2,1)}, f32[64,640]{1,0:T(8,128)}, f32[64,640]{1,0:T(8,128)}) custom-call(s32[4]{0:T(128)} %lengths.1, bf16[160,640]{1,0:T(8,128)(2,1)} %q_hbm.1, bf16[160,128]{1,0:T(8,128)(2,1)} %k_hbm.1, bf16[160,128]{1,0:T(8,128)(2,1)} %v_hbm.1, ...), custom_call_target="tpu_custom_call" | custom-call | tf_op jit(solution)/shard_map/pallas_call | solution.py:477
  55.7 1.9 %shard_map.120 = (bf16[160,640]{1,0:T(8,128)(2,1)}, bf16[160,128]{1,0:T(8,128)(2,1)}, bf16[160,128]{1,0:T(8,128)(2,1)}, f32[64,640]{1,0:T(8,128)}, f32[64,640]{1,0:T(8,128)}) custom-call(bf16[160,640]{1,0:T(8,128)(2,1)} %get-tuple-element.15.refs_0_, bf16[160,128]{1,0:T(8,128)(2,1)} %get-tuple-element.16.refs_1_, ...), custom_call_target="tpu_custom_call" | custom-call | tf_op jit(solution)/shard_map/pallas_call | solution.py:517
where the time goes:
time: 58.3 us; the launch traced here: 57.5 us
  Pallas kernels  56.9 us (98%)
  between operations  0.64 us (1%)
    pallas_call x1, Pallas kernels, body(): pl.pallas_call(kernel, out_shape=shapes, in_specs=[pl.BlockSpec(memory_sp...  55 us
    pallas_call x1, Pallas kernels, body(): pl.pallas_call(hand_on, out_shape=shapes, in_specs=[hbm] * 5, out_specs=(...  1.89 us

commit v1 on v0

--- a/solution.py
+++ b/solution.py
@@ -88,8 +88,8 @@
     for kind in (0, 1):
         kv[slot(kind, y, c)] = jnp.zeros((T, 2 * HEAD_SIZE), BF16)
     barrier = pltpu.get_barrier_semaphore()
-    plane = [(d, cc) for d in (0, 1, 2, 3) for cc in (0, 1) if (d, cc) != (0, 0)]
-    ranks = [along(dx=d) for d in (1, 2, 3)] + [along(dx=d, z=1 - zl) for d in (0, 1, 2, 3)]
+    plane = [(d, cc) for d in (2, 1, 3, 0) for cc in (0, 1) if (d, cc) != (0, 0)]
+    ranks = [along(dx=d) for d in (2, 1, 3)] + [along(dx=d, z=1 - zl) for d in (2, 1, 3, 0)]
     partners = [at(dh=d) for d in (2, 1, 3)] + ranks + [at(dy=d, core=(c + cc) % 2) for d, cc in plane]
     for partner in partners:
         pl.semaphore_signal(barrier, inc=1, device_id=partner, device_id_type=MESH)
@@ -133,7 +133,7 @@
     send(half(mp, 0), half(mp, 0), COT + 0, along(z=1 - zl))
     send(half(mp, 1), half(mp, 1), COT + 1, along(z=1 - zl))
     early, late = [], []
-    for d in (1, 2, 3):
+    for d in (2, 1, 3):
         copy = message_to(kv.at[16], kv.at[mix], KV + mix, at(dy=d))
         early.append((y + d < 4, copy))
         late.append((y + d >= 4, pltpu.make_async_remote_copy(
@@ -217,7 +217,7 @@
     arrived(half(right + zl, 1), COT + 5)
     send(half(right + zl, 1), half(right + zl, 1), COT + 7, along(dx=-1))
     pl.when(h >= 1)(lambda: arrived(kv.at[g1], KV + g1))
-    for d in (1, 2, 3):
+    for d in (2, 1, 3):
         send(kv.at[g1], kv.at[g1], KV + g1, at(dy=d))
     send(kv.at[g1], kv.at[g1], KV + g1, at(core=other))
     pl.when(h >= 2)(lambda: arrived(kv.at[mix], KV + mix))
@@ -235,7 +235,7 @@
     project(near)
 
     for kind in (0, 1):
-        for d in (1, 2, 3):
+        for d in (2, 1, 3):
             s = slot(kind, (y + d) % 4, c)
             arrived(kv.at[s], KV + s)
             send(kv.at[s], kv.at[s], KV + s, at(core=other))
@@ -329,7 +329,7 @@
         for yy in range(4):
             n = 4 * kind + yy
             arrived(sib.at[kv_of, n], SIB + 8 * kv_of + n)
-        for d in (1, 2, 3):
+        for d in (2, 1, 3):
             yy = (y + d) % 4
             s = slot(kind, yy, c)
             parts[kv_of, s] = (parts[kv_of, s].astype(F32) + sib[kv_of, 4 * kind + yy].astype(F32)).astype(BF16)
@@ -345,7 +345,7 @@
     def along_z(kv_of, kind):
         s = mix if kind == 1 else g1
         total = parts[kv_of, s].astype(F32)
-        for d in (1, 2, 3):
+        for d in (2, 1, 3):
             n = 6 * kv_of + 3 * kind + d - 1
             arrived(col.at[n], COL + n)
             term = col[n].astype(F32)
@@ -397,7 +397,7 @@
         arrived(du_in.at[n], DU + n)
         total_du = total_du + du_in[n].astype(F32)
     du_z[3] = total_du.astype(BF16)
-    for d in (1, 2, 3):
+    for d in (2, 1, 3):
         send(du_z.at[3], du_z.at[d - 1], DU_Z + d - 1, at(dh=d))
 
     for kind in (1, 0):
@@ -406,7 +406,7 @@
         dq_t = key_part(*by_key[kind, 0], dq_t)
         along_y(0, kind)
 
-    for d in (1, 2, 3):
+    for d in (2, 1, 3):
         arrived(du_z.at[d - 1], DU_Z + d - 1)
         total_du = total_du + du_z[d - 1].astype(F32)
     du_sum[piece(y, c)] = total_du.astype(BF16)

time: 58.3 us -> 57.8 us (level)
  Pallas kernels: 56.9 us -> 56 us
    pallas_call x1, Pallas kernels: 55 us -> 54.1 us  [body(): pl.pallas_call(kernel, out_shape=shapes, in_specs=[pl.BlockSpec(memory_sp...]
where the time goes in v1:
time: 57.8 us; the launch traced here: 56.6 us
  Pallas kernels  56 us (97%)
  between operations  0.64 us (1%)
    pallas_call x1, Pallas kernels, body(): pl.pallas_call(kernel, out_shape=shapes, in_specs=[pl.BlockSpec(memory_sp...  54.1 us
    pallas_call x1, Pallas kernels, body(): pl.pallas_call(hand_on, out_shape=shapes, in_specs=[hbm] * 5, out_specs=(...  1.89 us

profile of v1, /device:TPU:1, one launch (start us, length us, event | category | flops | bytes accessed | tf_op | source)
XLA Modules:
  0.0 56.6 jit_solution(12628628601642423298)
XLA Ops:
  0.6 54.1 %shard_map.119 = (bf16[160,640]{1,0:T(8,128)(2,1)}, bf16[160,128]{1,0:T(8,128)(2,1)}, bf16[160,128]{1,0:T(8,128)(2,1)}, f32[64,640]{1,0:T(8,128)}, f32[64,640]{1,0:T(8,128)}) custom-call(s32[4]{0:T(128)} %lengths.1, bf16[160,640]{1,0:T(8,128)(2,1)} %q_hbm.1, bf16[160,128]{1,0:T(8,128)(2,1)} %k_hbm.1, bf16[160,128]{1,0:T(8,128)(2,1)} %v_hbm.1, ...), custom_call_target="tpu_custom_call" | custom-call | tf_op jit(solution)/shard_map/pallas_call | solution.py:477
  54.7 1.9 %shard_map.120 = (bf16[160,640]{1,0:T(8,128)(2,1)}, bf16[160,128]{1,0:T(8,128)(2,1)}, bf16[160,128]{1,0:T(8,128)(2,1)}, f32[64,640]{1,0:T(8,128)}, f32[64,640]{1,0:T(8,128)}) custom-call(bf16[160,640]{1,0:T(8,128)(2,1)} %get-tuple-element.15.refs_0_, bf16[160,128]{1,0:T(8,128)(2,1)} %get-tuple-element.16.refs_1_, ...), custom_call_target="tpu_custom_call" | custom-call | tf_op jit(solution)/shard_map/pallas_call | solution.py:517
